TPU v7x, 32 devices: a whole 2x2x4 slice. The times are simulated.
32 devices in a mesh: groups: 2 (over y), rows: 4 (over z), cols: 2 (over x), date: 2 (over core).
Axes of the slice: x: 2, y: 2, z: 4, core: 2. Of those that a mesh axis runs over, the one named last changes fastest.
Arguments:
- features: bfloat16 [2, 128, 256, 128], P('date', ('groups', 'rows'), 'cols'), parts along dimension 1, may hold values from -6 to 6
- scene_shift: int32 [8, 2, 2], P('groups'), parts along dimension 0, may hold values from -4 to 4, as said below
- w_lat: bfloat16 [128, 128], replicated, may hold values from -0.5 to 0.5
- b_lat: float32 [128], replicated, may hold values from -3 to 3
- w_fpn: bfloat16 [3, 3, 128, 128], replicated, may hold values from -0.1875 to 0.1875
- w_dec1: bfloat16 [3, 3, 128, 128], replicated, may hold values from -0.1875 to 0.1875
- b_dec1: float32 [128], replicated, may hold values from -3 to 3
- w_dec2: bfloat16 [3, 3, 128, 128], replicated, may hold values from -0.1875 to 0.1875
- b_dec2: float32 [128], replicated, may hold values from -3 to 3
- w_out: bfloat16 [128], replicated, may hold values from -0.5 to 0.5
- b_out: float32 [1], replicated, may hold values from -3 to 3
Outputs:
- change_logit: float32 [128, 256], P(('groups', 'rows', 'date'), 'cols'), parts along dimension 0
There are 2 independent parts, one for each index of `groups`. A program takes and returns all parts, laid end to end along the dimension named above; an argument that names none is the same for every part. Nothing has to cross between parts.
Inputs may be any that keep to these rules, and one draw needn't show every extreme that they name: `scene_shift`: each offset component lies between -4 and 4; 4 and -4 both occur in every draw.
All inputs are finite; a program needn't handle non-finite values.
Results may differ from a plain program's by a relative error of at most 0.0076.
Values may be sent and summed in bfloat16 or wider, within the bound.
A program may use at most 64 MiB of HBM per device.

v0:
```python
import jax
import jax.numpy as jnp
from jax import lax
from jax.sharding import PartitionSpec as P

MO = 4


def extended(x, sides, width):
    for axis, dim in sides:
        size, length = (lax.axis_size(axis), x.shape[dim])
        up = [(i, (i + 1) % size) for i in range(size - 1)]
        down = [(j, i) for i, j in up]
        last = lax.slice_in_dim(x, length - width, length, axis=dim)
        first = lax.slice_in_dim(x, 0, width, axis=dim)
        before = lax.ppermute(last, axis, up)
        after = lax.ppermute(first, axis, down)
        x = jnp.concatenate([before, x, after], axis=dim)
    return x


def from_partner(value, axis, bit):
    mask = 2**bit
    pairs = [(source, source ^ mask) for source in range(lax.axis_size(axis))]
    return lax.ppermute(value, axis, pairs)


def conv_three(padded, weights):
    out_rows = padded.shape[0] - 2
    out_cols = padded.shape[1] - 2
    channels = padded.shape[2]
    total = jnp.zeros((out_rows * out_cols, weights.shape[3]), jnp.float32)
    for row_tap in range(3):
        for col_tap in range(3):
            window = padded[row_tap : row_tap + out_rows, col_tap : col_tap + out_cols].reshape(
                -1, channels
            )
            total = total + jnp.dot(
                window, weights[row_tap, col_tap], preferred_element_type=jnp.float32
            )
    return total.reshape(out_rows, out_cols, weights.shape[3])


def lateral_map(inputs, w_lat, b_lat):
    flat = (
        jnp.dot(inputs.reshape(-1, inputs.shape[-1]), w_lat, preferred_element_type=jnp.float32)
        + b_lat
    )
    return flat.astype(jnp.bfloat16).reshape(inputs.shape[:-1] + (w_lat.shape[1],))


def grid_mask(cycle, half_rows, tile_cols):
    global_row = (
        lax.axis_index(("rows", "date")) * half_rows - cycle + jnp.arange(half_rows + 2 * cycle)
    )
    global_col = lax.axis_index("cols") * tile_cols - cycle + jnp.arange(tile_cols + 2 * cycle)
    row_valid = (global_row >= 0) & (global_row < lax.axis_size(("rows", "date")) * half_rows)
    col_valid = (global_col >= 0) & (global_col < lax.axis_size("cols") * tile_cols)
    return (row_valid[:, None] & col_valid[None, :]).astype(jnp.float32)


def regrid(rim, half_rows, tile_cols, scene_shift, margin, extra):
    channels = rim.shape[2]
    width = margin + extra
    offset_base = width + margin
    place_row = lax.axis_index(("rows", "date"))
    place_col = lax.axis_index("cols")
    row_total = lax.axis_size(("rows", "date"))
    col_total = lax.axis_size("cols")
    date_total = lax.axis_size("date")
    canvas = jnp.zeros(
        (half_rows + 2 * offset_base, tile_cols + 2 * offset_base, channels), jnp.float32
    )
    counts = jnp.zeros((half_rows + 2 * offset_base, tile_cols + 2 * offset_base), jnp.float32)
    row_parts = (
        (-1, 0, width, half_rows - width),
        (0, width, half_rows, 0),
        (1, width + half_rows, width, 0),
    )
    col_parts = (
        (-1, 0, width, tile_cols - width),
        (0, width, tile_cols, 0),
        (1, width + tile_cols, width, 0),
    )
    zero = jnp.zeros((), jnp.int32)
    for row_step, row_from, row_len, row_start in row_parts:
        for col_step, col_from, col_len, col_start in col_parts:
            near_row = place_row + row_step
            near_col = place_col + col_step
            inside = (
                (near_row >= 0) & (near_row < row_total) & (near_col >= 0) & (near_col < col_total)
            )
            scene_row = jnp.clip(near_row, 0, row_total - 1) // date_total
            scene_col = jnp.clip(near_col, 0, col_total - 1)
            offset = scene_shift[scene_row, scene_col]
            top = row_step * half_rows + row_start + offset_base + offset[0]
            left = col_step * tile_cols + col_start + offset_base + offset[1]
            present = inside.astype(jnp.float32)
            piece = (
                rim[row_from : row_from + row_len, col_from : col_from + col_len].astype(
                    jnp.float32
                )
                * present
            )
            region = lax.dynamic_slice(canvas, (top, left, zero), (row_len, col_len, channels))
            canvas = lax.dynamic_update_slice(canvas, region + piece, (top, left, zero))
            region_count = lax.dynamic_slice(counts, (top, left), (row_len, col_len))
            counts = lax.dynamic_update_slice(counts, region_count + present, (top, left))
    low = offset_base - extra
    b_sum = canvas[low : low + half_rows + 2 * extra, low : low + tile_cols + 2 * extra]
    coverage = counts[low : low + half_rows + 2 * extra, low : low + tile_cols + 2 * extra]
    return (b_sum, coverage)


def per_device(
    features, scene_shift, w_lat, b_lat, w_fpn, w_dec1, b_dec1, w_dec2, b_dec2, w_out, b_out
):
    tile_rows = features.shape[1]
    tile_cols = features.shape[2]
    half_rows = tile_rows // 2
    which_date = lax.axis_index("date")
    is_first = which_date == 0
    lateral = lateral_map(features[0], w_lat, b_lat)
    padded = extended(lateral, (("rows", 0), ("cols", 1)), 1)
    pyramid = conv_three(padded, w_fpn).astype(jnp.bfloat16)
    kept_part = lax.dynamic_slice_in_dim(pyramid, which_date * half_rows, half_rows, 0)
    sent_part = lax.dynamic_slice_in_dim(pyramid, (1 - which_date) * half_rows, half_rows, 0)
    received = from_partner(sent_part, "date", 0)
    a_half = jnp.where(is_first, kept_part, received)
    b_half = jnp.where(is_first, received, kept_part)
    extra = 0
    rim = extended(b_half, ((("rows", "date"), 0), ("cols", 1)), MO + extra)
    b_sum, coverage = regrid(rim, half_rows, tile_cols, scene_shift, MO, extra)
    covered = jnp.minimum(coverage, 1.0)[:, :, None]
    regridded = b_sum / jnp.maximum(coverage, 1.0)[:, :, None]
    difference = (jnp.abs(a_half.astype(jnp.float32) - regridded) * covered).astype(jnp.bfloat16)
    padded_diff = extended(difference, ((("rows", "date"), 0), ("cols", 1)), 2)
    wide_hidden = jnp.maximum(conv_three(padded_diff, w_dec1) + b_dec1, 0.0)
    inside = grid_mask(1, half_rows, tile_cols)
    hidden_one = (wide_hidden * inside[:, :, None]).astype(jnp.bfloat16)
    hidden_two = jnp.maximum(conv_three(hidden_one, w_dec2) + b_dec2, 0.0).astype(jnp.bfloat16)
    logit = (
        jnp.dot(
            hidden_two.reshape(-1, hidden_two.shape[2]), w_out, preferred_element_type=jnp.float32
        )
        + b_out
    )
    return logit.reshape(half_rows, tile_cols)


def solution(mesh):
    return jax.shard_map(
        per_device,
        mesh=mesh,
        in_specs=(
            P("date", ("groups", "rows"), "cols", None),
            P("groups", None, None),
            P(),
            P(),
            P(),
            P(),
            P(),
            P(),
            P(),
            P(),
            P(),
        ),
        out_specs=P(("groups", "rows", "date"), "cols"),
        check_vma=False,
    )
```

profile of v0, /device:TPU:12, one launch (start us, length us, event | category | flops | bytes accessed | tf_op | source)
XLA Modules:
  0.0 105.2 jit_solution(506069014609525896)
XLA Ops:
  0.0 1.0 copy-done
  1.0 1.1 %fusion.1 = bf16[2048,128]{1,0:T(8,128)(2,1)S(1)} fusion(bf16[2048,128]{1,0:T(8,128)(2,1)S(1)} %bitcast.179, bf16[128,128]{1,0:T(8,128)(2,1)} %param.13, f32[128]{0:T(128)} %param.14), kind=kOutput, calls=%fused_computation.17 | convolution fusion | flops 67633152 | bytes 1081856 | tf_op jit(solution)/shard_map/dot_general | solution.py:46
  2.1 3.5 %collective-permute-start = (bf16[1,128,128]{2,1,0:T(8,128)(2,1)S(1)}, bf16[1,128,128]{2,1,0:T(8,128)(2,1)S(1)}, u32[]{:S(2)}, u32[]{:S(2)}) collective-permute-start(bf16[1,128,128]{2,1,0:T(8,128)(2,1)S(1)} %get-tuple-element.19), channel_id=1, source_target_pairs={{0,4},{4,8},{8,12},{1,5},{5,9},{9,13},{2,6},{6,10},{10,14},{3,7},{... | collective-permute-start | bytes 98312 | tf_op jit(solution)/shard_map/ppermute | solution.py:16
  5.6 2.3 %collective-permute-start.1 = (bf16[1,128,128]{2,1,0:T(8,128)(2,1)S(1)}, bf16[1,128,128]{2,1,0:T(8,128)(2,1)S(1)}, u32[]{:S(2)}, u32[]{:S(2)}) collective-permute-start(bf16[1,128,128]{2,1,0:T(8,128)(2,1)S(1)} %get-tuple-element.20), channel_id=1, source_target_pairs={{4,0},{8,4},{12,8},{5,1},{9,5},{13,9},{6,2},{10,6},{14,10},{7,3},{... | collective-permute-start | bytes 98312 | tf_op jit(solution)/shard_map/ppermute | solution.py:17
  8.1 1.0 constant_dynamic-slice_fusion
  9.0 0.5 fusion.91
  10.9 0.6 fusion.89
  15.2 0.6 fusion.87
  22.3 0.6 fusion.85
  26.8 0.7 dynamic_update_slice.63
  27.5 0.6 dynamic_update_slice.64
  28.3 0.5 dynamic_update_slice.65
  28.9 0.6 dynamic_update_slice.66
  29.6 0.6 dynamic_update_slice.67
  30.2 0.6 fusion.83
  32.3 0.6 dynamic_update_slice.68
  34.1 3.4 %collective-permute-start.2 = (bf16[18,1,128]{2,1,0:T(2,128)(2,1)S(1)}, bf16[18,1,128]{2,1,0:T(2,128)(2,1)S(1)}, u32[]{:S(2)}, u32[]{:S(2)}) collective-permute-start(bf16[18,1,128]{2,1,0:T(2,128)(2,1)S(1)} %get-tuple-element.13), channel_id=1, source_target_pairs={{0,2},{1,3},{4,6},{5,7},{8,10},{9,11},{12,14},{13,15},{16,18},{17,... | collective-permute-start | bytes 13832 | tf_op jit(solution)/shard_map/ppermute | solution.py:16
  37.5 1.3 %collective-permute-start.3 = (bf16[18,1,128]{2,1,0:T(2,128)(2,1)S(1)}, bf16[18,1,128]{2,1,0:T(2,128)(2,1)S(1)}, u32[]{:S(2)}, u32[]{:S(2)}) collective-permute-start(bf16[18,1,128]{2,1,0:T(2,128)(2,1)S(1)} %get-tuple-element.14), channel_id=1, source_target_pairs={{2,0},{3,1},{6,4},{7,5},{10,8},{11,9},{14,12},{15,13},{18,16},{19,... | collective-permute-start | bytes 13832 | tf_op jit(solution)/shard_map/ppermute | solution.py:17
  39.2 3.9 %collective-permute-done.3 = bf16[18,1,128]{2,1,0:T(2,128)(2,1)S(1)} collective-permute-done((bf16[18,1,128]{2,1,0:T(2,128)(2,1)S(1)}, bf16[18,1,128]{2,1,0:T(2,128)(2,1)S(1)}, u32[]{:S(2)}, u32[]{:S(2)}) %collective-permute-start.3) | collective-permute-done | bytes 4640 | tf_op jit(solution)/shard_map/ppermute | solution.py:17
  43.1 0.3 maximum_maximum_fusion
  43.4 0.5 fusion.75
  44.2 0.3 convolution_add_fusion.13
  45.4 0.3 convolution_add_fusion.10
  45.9 0.3 fusion.2
  51.3 0.7 dynamic_update_slice.69
  52.1 0.6 dynamic_update_slice.70
  52.8 0.5 dynamic_update_slice.71
  53.4 2.4 %collective-permute-start.5 = (bf16[4,128,128]{2,1,0:T(8,128)(2,1)S(1)}, bf16[4,128,128]{2,1,0:T(8,128)(2,1)S(1)}, u32[]{:S(2)}, u32[]{:S(2)}) collective-permute-start(bf16[4,128,128]{2,1,0:T(8,128)(2,1)S(1)} %get-tuple-element.45), channel_id=1, source_target_pairs={{0,1},{1,4},{4,5},{5,8},{8,9},{9,12},{12,13},{2,3},{3,6},{6,7},{7,... | collective-permute-start | bytes 393224 | tf_op jit(solution)/shard_map/ppermute | solution.py:16
  55.8 3.2 %collective-permute-start.6 = (bf16[4,128,128]{2,1,0:T(8,128)(2,1)S(1)}, bf16[4,128,128]{2,1,0:T(8,128)(2,1)S(1)}, u32[]{:S(2)}, u32[]{:S(2)}) collective-permute-start(bf16[4,128,128]{2,1,0:T(8,128)(2,1)S(1)} %get-tuple-element.46), channel_id=1, source_target_pairs={{1,0},{4,1},{5,4},{8,5},{9,8},{12,9},{13,12},{3,2},{6,3},{7,6},{10... | collective-permute-start | bytes 393224 | tf_op jit(solution)/shard_map/ppermute | solution.py:17
  59.1 0.6 collective-permute-done.5
  59.7 1.8 %collective-permute-done.6 = bf16[4,128,128]{2,1,0:T(8,128)(2,1)S(1)} collective-permute-done((bf16[4,128,128]{2,1,0:T(8,128)(2,1)S(1)}, bf16[4,128,128]{2,1,0:T(8,128)(2,1)S(1)}, u32[]{:S(2)}, u32[]{:S(2)}) %collective-permute-start.6) | collective-permute-done | bytes 131104 | tf_op jit(solution)/shard_map/ppermute | solution.py:17
  61.5 1.6 %collective-permute-start.7 = (bf16[16,4,128]{2,1,0:T(4,128)(2,1)S(1)}, bf16[16,4,128]{2,1,0:T(4,128)(2,1)S(1)}, u32[]{:S(2)}, u32[]{:S(2)}) collective-permute-start(bf16[16,4,128]{2,1,0:T(4,128)(2,1)S(1)} %get-tuple-element.16), channel_id=1, source_target_pairs={{0,2},{1,3},{4,6},{5,7},{8,10},{9,11},{12,14},{13,15},{16,18},{17,... | collective-permute-start | bytes 49160 | tf_op jit(solution)/shard_map/ppermute | solution.py:16
  63.2 1.3 %collective-permute-start.8 = (bf16[16,4,128]{2,1,0:T(4,128)(2,1)S(1)}, bf16[16,4,128]{2,1,0:T(4,128)(2,1)S(1)}, u32[]{:S(2)}, u32[]{:S(2)}) collective-permute-start(bf16[16,4,128]{2,1,0:T(4,128)(2,1)S(1)} %get-tuple-element.15), channel_id=1, source_target_pairs={{2,0},{3,1},{6,4},{7,5},{10,8},{11,9},{14,12},{15,13},{18,16},{19,... | collective-permute-start | bytes 49160 | tf_op jit(solution)/shard_map/ppermute | solution.py:17
  64.9 1.0 multiply_add_fusion.2
  65.8 0.5 dynamic_update_slice.55
  66.3 2.5 %collective-permute-done.8 = bf16[16,4,128]{2,1,0:T(4,128)(2,1)S(1)} collective-permute-done((bf16[16,4,128]{2,1,0:T(4,128)(2,1)S(1)}, bf16[16,4,128]{2,1,0:T(4,128)(2,1)S(1)}, u32[]{:S(2)}, u32[]{:S(2)}) %collective-permute-start.8) | collective-permute-done | bytes 16416 | tf_op jit(solution)/shard_map/ppermute | solution.py:17
  69.2 0.9 multiply_add_fusion
  70.1 2.7 %dynamic_update_slice.58 = f32[24,144,128]{2,1,0:T(8,128)S(1)} dynamic-update-slice(f32[24,144,128]{2,1,0:T(8,128)S(1)} %dynamic_update_slice.57, f32[8,128,128]{2,1,0:T(8,128)} %multiply_add_fusion, s32[]{:T(128)S(6)} %select_n.92, s32[]{:T(128)S(6)} %select_n.93, s32[]{:T(128)} %constant.131.clone.1) | dynamic-update-slice | bytes 1048580 | tf_op jit(solution)/shard_map/dynamic_update_slice | solution.py:106
  73.2 0.5 dynamic_update_slice.61
  73.8 0.3 fusion.10
  74.2 2.4 %collective-permute-start.10 = (bf16[2,128,128]{2,1,0:T(8,128)(2,1)S(1)}, bf16[2,128,128]{2,1,0:T(8,128)(2,1)S(1)}, u32[]{:S(2)}, u32[]{:S(2)}) collective-permute-start(bf16[2,128,128]{2,1,0:T(8,128)(2,1)S(1)} %get-tuple-element.44), channel_id=1, source_target_pairs={{1,0},{4,1},{5,4},{8,5},{9,8},{12,9},{13,12},{3,2},{6,3},{7,6},{10... | collective-permute-start | bytes 196616 | tf_op jit(solution)/shard_map/ppermute | solution.py:17
  76.6 2.0 %collective-permute-start.9 = (bf16[2,128,128]{2,1,0:T(8,128)(2,1)S(1)}, bf16[2,128,128]{2,1,0:T(8,128)(2,1)S(1)}, u32[]{:S(2)}, u32[]{:S(2)}) collective-permute-start(bf16[2,128,128]{2,1,0:T(8,128)(2,1)S(1)} %get-tuple-element.43), channel_id=1, source_target_pairs={{0,1},{1,4},{4,5},{5,8},{8,9},{9,12},{12,13},{2,3},{3,6},{6,7},{7,... | collective-permute-start | bytes 196616 | tf_op jit(solution)/shard_map/ppermute | solution.py:16
  78.6 3.6 %collective-permute-done.9 = bf16[2,128,128]{2,1,0:T(8,128)(2,1)S(1)} collective-permute-done((bf16[2,128,128]{2,1,0:T(8,128)(2,1)S(1)}, bf16[2,128,128]{2,1,0:T(8,128)(2,1)S(1)}, u32[]{:S(2)}, u32[]{:S(2)}) %collective-permute-start.9) | collective-permute-done | bytes 65568 | tf_op jit(solution)/shard_map/ppermute | solution.py:16
  82.2 2.9 %collective-permute-start.11 = (bf16[12,2,128]{2,1,0:T(2,128)(2,1)S(1)}, bf16[12,2,128]{2,1,0:T(2,128)(2,1)S(1)}, u32[]{:S(2)}, u32[]{:S(2)}) collective-permute-start(bf16[12,2,128]{2,1,0:T(2,128)(2,1)S(1)} %get-tuple-element.32), channel_id=1, source_target_pairs={{0,2},{1,3},{4,6},{5,7},{8,10},{9,11},{12,14},{13,15},{16,18},{17,... | collective-permute-start | bytes 18440 | tf_op jit(solution)/shard_map/ppermute | solution.py:16
  85.0 1.5 %collective-permute-start.12 = (bf16[12,2,128]{2,1,0:T(2,128)(2,1)S(1)}, bf16[12,2,128]{2,1,0:T(2,128)(2,1)S(1)}, u32[]{:S(2)}, u32[]{:S(2)}) collective-permute-start(bf16[12,2,128]{2,1,0:T(2,128)(2,1)S(1)} %get-tuple-element.33), channel_id=1, source_target_pairs={{2,0},{3,1},{6,4},{7,5},{10,8},{11,9},{14,12},{15,13},{18,16},{19,... | collective-permute-start | bytes 18440 | tf_op jit(solution)/shard_map/ppermute | solution.py:17
  87.3 3.3 %collective-permute-done.12 = bf16[12,2,128]{2,1,0:T(2,128)(2,1)S(1)} collective-permute-done((bf16[12,2,128]{2,1,0:T(2,128)(2,1)S(1)}, bf16[12,2,128]{2,1,0:T(2,128)(2,1)S(1)}, u32[]{:S(2)}, u32[]{:S(2)}) %collective-permute-start.12) | collective-permute-done | bytes 6176 | tf_op jit(solution)/shard_map/ppermute | solution.py:17
  90.9 0.8 reshape.257
  92.0 0.8 reshape.258
  92.9 0.8 reshape.259
  93.7 0.8 reshape.260
  95.1 0.5 copy-done.2
  95.6 1.1 %fusion.31 = f32[1300,128]{1,0:T(8,128)S(1)} fusion(bf16[1300,128]{1,0:T(8,128)(2,1)S(1)} %copy-done.2, bf16[3,3,128,128]{3,2,1,0:T(8,128)(2,1)} %param.16), kind=kOutput, calls=%fused_computation.69 | convolution fusion | flops 42598400 | bytes 1031168 | tf_op jit(solution)/shard_map/dot_general | solution.py:38
  96.7 1.1 %convolution_add_fusion.7 = f32[1300,128]{1,0:T(8,128)S(1)} fusion(f32[1300,128]{1,0:T(8,128)S(1)} %fusion.31, bf16[1300,128]{1,0:T(8,128)(2,1)S(1)} %copy-done.1, bf16[3,3,128,128]{3,2,1,0:T(8,128)(2,1)} %param.16), kind=kOutput, calls=%fused_computation.7 | convolution fusion | flops 42764800 | bytes 1696768 | tf_op jit(solution)/shard_map/dot_general | solution.py:38
  97.9 1.1 %convolution_add_fusion.6 = f32[1300,128]{1,0:T(8,128)S(1)} fusion(f32[1300,128]{1,0:T(8,128)S(1)} %convolution_add_fusion.7, bf16[1300,128]{1,0:T(8,128)(2,1)S(1)} %copy-done.4, bf16[3,3,128,128]{3,2,1,0:T(8,128)(2,1)} %param.16), kind=kOutput, calls=%fused_computation.6 | convolution fusion | flops 42764800 | bytes 1696768 | tf_op jit(solution)/shard_map/dot_general | solution.py:38
  99.0 0.3 convolution_add_fusion.5
  99.3 0.3 convolution_add_fusion.4
  99.6 0.3 convolution_add_fusion.3
  99.9 0.3 convolution_add_fusion.2
  100.2 0.3 convolution_add_fusion.1
  100.6 0.3 convolution_add_fusion
  101.5 0.4 fusion.80
  101.9 0.5 copy-done.9
  104.2 0.4 fusion.6
  104.6 0.6 add_bitcast_fusion
  (96 shorter events, 7.5 us)
Async XLA Ops:
  0.0 1.0 copy-start
  1.0 37.9 %copy-start.8 = (bf16[3,3,128,128]{3,2,1,0:T(8,128)(2,1)S(1)}, bf16[3,3,128,128]{3,2,1,0:T(8,128)(2,1)}, u32[]{:S(2)}) copy-start(bf16[3,3,128,128]{3,2,1,0:T(8,128)(2,1)} %param.15) | copy-start | bytes 884740
  2.1 31.9 %collective-permute-start = (bf16[1,128,128]{2,1,0:T(8,128)(2,1)S(1)}, bf16[1,128,128]{2,1,0:T(8,128)(2,1)S(1)}, u32[]{:S(2)}, u32[]{:S(2)}) collective-permute-start(bf16[1,128,128]{2,1,0:T(8,128)(2,1)S(1)} %get-tuple-element.19), channel_id=1, source_target_pairs={{0,4},{4,8},{8,12},{1,5},{5,9},{9,13},{2,6},{6,10},{10,14},{3,7},{... | collective-permute-start | bytes 98312 | tf_op jit(solution)/shard_map/ppermute | solution.py:16
  5.6 28.5 %collective-permute-start.1 = (bf16[1,128,128]{2,1,0:T(8,128)(2,1)S(1)}, bf16[1,128,128]{2,1,0:T(8,128)(2,1)S(1)}, u32[]{:S(2)}, u32[]{:S(2)}) collective-permute-start(bf16[1,128,128]{2,1,0:T(8,128)(2,1)S(1)} %get-tuple-element.20), channel_id=1, source_target_pairs={{4,0},{8,4},{12,8},{5,1},{9,5},{13,9},{6,2},{10,6},{14,10},{7,3},{... | collective-permute-start | bytes 98312 | tf_op jit(solution)/shard_map/ppermute | solution.py:17
  34.1 5.1 %collective-permute-start.2 = (bf16[18,1,128]{2,1,0:T(2,128)(2,1)S(1)}, bf16[18,1,128]{2,1,0:T(2,128)(2,1)S(1)}, u32[]{:S(2)}, u32[]{:S(2)}) collective-permute-start(bf16[18,1,128]{2,1,0:T(2,128)(2,1)S(1)} %get-tuple-element.13), channel_id=1, source_target_pairs={{0,2},{1,3},{4,6},{5,7},{8,10},{9,11},{12,14},{13,15},{16,18},{17,... | collective-permute-start | bytes 13832 | tf_op jit(solution)/shard_map/ppermute | solution.py:16
  37.5 5.6 %collective-permute-start.3 = (bf16[18,1,128]{2,1,0:T(2,128)(2,1)S(1)}, bf16[18,1,128]{2,1,0:T(2,128)(2,1)S(1)}, u32[]{:S(2)}, u32[]{:S(2)}) collective-permute-start(bf16[18,1,128]{2,1,0:T(2,128)(2,1)S(1)} %get-tuple-element.14), channel_id=1, source_target_pairs={{2,0},{3,1},{6,4},{7,5},{10,8},{11,9},{14,12},{15,13},{18,16},{19,... | collective-permute-start | bytes 13832 | tf_op jit(solution)/shard_map/ppermute | solution.py:17
  46.3 7.1 %collective-permute-start.4 = (bf16[8,128,128]{2,1,0:T(8,128)(2,1)S(1)}, bf16[8,128,128]{2,1,0:T(8,128)(2,1)S(1)}, u32[]{:S(2)}, u32[]{:S(2)}) collective-permute-start(bf16[8,128,128]{2,1,0:T(8,128)(2,1)S(1)} %constant_dynamic-slice_fusion.9), channel_id=1, source_target_pairs={{0,1},{1,0},{2,3},{3,2},{4,5},{5,4},{6,7},{7,6},{8,9},{9,8},{10,11... | collective-permute-start | bytes 786440 | tf_op jit(solution)/shard_map/ppermute | solution.py:25
  53.3 11.3 %copy-start.5 = (bf16[8,128,128]{2,1,0:T(8,128)(2,1)}, bf16[8,128,128]{2,1,0:T(8,128)(2,1)S(1)}, u32[]{:S(2)}) copy-start(bf16[8,128,128]{2,1,0:T(8,128)(2,1)S(1)} %collective-permute-done.4) | copy-start | bytes 786436
  53.4 6.3 %collective-permute-start.5 = (bf16[4,128,128]{2,1,0:T(8,128)(2,1)S(1)}, bf16[4,128,128]{2,1,0:T(8,128)(2,1)S(1)}, u32[]{:S(2)}, u32[]{:S(2)}) collective-permute-start(bf16[4,128,128]{2,1,0:T(8,128)(2,1)S(1)} %get-tuple-element.45), channel_id=1, source_target_pairs={{0,1},{1,4},{4,5},{5,8},{8,9},{9,12},{12,13},{2,3},{3,6},{6,7},{7,... | collective-permute-start | bytes 393224 | tf_op jit(solution)/shard_map/ppermute | solution.py:16
  55.8 5.7 %collective-permute-start.6 = (bf16[4,128,128]{2,1,0:T(8,128)(2,1)S(1)}, bf16[4,128,128]{2,1,0:T(8,128)(2,1)S(1)}, u32[]{:S(2)}, u32[]{:S(2)}) collective-permute-start(bf16[4,128,128]{2,1,0:T(8,128)(2,1)S(1)} %get-tuple-element.46), channel_id=1, source_target_pairs={{1,0},{4,1},{5,4},{8,5},{9,8},{12,9},{13,12},{3,2},{6,3},{7,6},{10... | collective-permute-start | bytes 393224 | tf_op jit(solution)/shard_map/ppermute | solution.py:17
  59.7 4.9 %copy-start.7 = (bf16[4,128,128]{2,1,0:T(8,128)(2,1)}, bf16[4,128,128]{2,1,0:T(8,128)(2,1)S(1)}, u32[]{:S(2)}) copy-start(bf16[4,128,128]{2,1,0:T(8,128)(2,1)S(1)} %collective-permute-done.5) | copy-start | bytes 393220
  61.5 3.1 %collective-permute-start.7 = (bf16[16,4,128]{2,1,0:T(4,128)(2,1)S(1)}, bf16[16,4,128]{2,1,0:T(4,128)(2,1)S(1)}, u32[]{:S(2)}, u32[]{:S(2)}) collective-permute-start(bf16[16,4,128]{2,1,0:T(4,128)(2,1)S(1)} %get-tuple-element.16), channel_id=1, source_target_pairs={{0,2},{1,3},{4,6},{5,7},{8,10},{9,11},{12,14},{13,15},{16,18},{17,... | collective-permute-start | bytes 49160 | tf_op jit(solution)/shard_map/ppermute | solution.py:16
  63.2 5.6 %collective-permute-start.8 = (bf16[16,4,128]{2,1,0:T(4,128)(2,1)S(1)}, bf16[16,4,128]{2,1,0:T(4,128)(2,1)S(1)}, u32[]{:S(2)}, u32[]{:S(2)}) collective-permute-start(bf16[16,4,128]{2,1,0:T(4,128)(2,1)S(1)} %get-tuple-element.15), channel_id=1, source_target_pairs={{2,0},{3,1},{6,4},{7,5},{10,8},{11,9},{14,12},{15,13},{18,16},{19,... | collective-permute-start | bytes 49160 | tf_op jit(solution)/shard_map/ppermute | solution.py:17
  69.2 4.6 %copy-start.6 = (bf16[8,128,128]{2,1,0:T(8,128)(2,1)S(1)}, bf16[8,128,128]{2,1,0:T(8,128)(2,1)}, u32[]{:S(2)}) copy-start(bf16[8,128,128]{2,1,0:T(8,128)(2,1)} %copy-done.5) | copy-start | bytes 786436
  74.2 4.4 %collective-permute-start.10 = (bf16[2,128,128]{2,1,0:T(8,128)(2,1)S(1)}, bf16[2,128,128]{2,1,0:T(8,128)(2,1)S(1)}, u32[]{:S(2)}, u32[]{:S(2)}) collective-permute-start(bf16[2,128,128]{2,1,0:T(8,128)(2,1)S(1)} %get-tuple-element.44), channel_id=1, source_target_pairs={{1,0},{4,1},{5,4},{8,5},{9,8},{12,9},{13,12},{3,2},{6,3},{7,6},{10... | collective-permute-start | bytes 196616 | tf_op jit(solution)/shard_map/ppermute | solution.py:17
  76.6 5.6 %collective-permute-start.9 = (bf16[2,128,128]{2,1,0:T(8,128)(2,1)S(1)}, bf16[2,128,128]{2,1,0:T(8,128)(2,1)S(1)}, u32[]{:S(2)}, u32[]{:S(2)}) collective-permute-start(bf16[2,128,128]{2,1,0:T(8,128)(2,1)S(1)} %get-tuple-element.43), channel_id=1, source_target_pairs={{0,1},{1,4},{4,5},{5,8},{8,9},{9,12},{12,13},{2,3},{3,6},{6,7},{7,... | collective-permute-start | bytes 196616 | tf_op jit(solution)/shard_map/ppermute | solution.py:16
  82.2 5.1 %collective-permute-start.11 = (bf16[12,2,128]{2,1,0:T(2,128)(2,1)S(1)}, bf16[12,2,128]{2,1,0:T(2,128)(2,1)S(1)}, u32[]{:S(2)}, u32[]{:S(2)}) collective-permute-start(bf16[12,2,128]{2,1,0:T(2,128)(2,1)S(1)} %get-tuple-element.32), channel_id=1, source_target_pairs={{0,2},{1,3},{4,6},{5,7},{8,10},{9,11},{12,14},{13,15},{16,18},{17,... | collective-permute-start | bytes 18440 | tf_op jit(solution)/shard_map/ppermute | solution.py:16
  85.0 5.5 %collective-permute-start.12 = (bf16[12,2,128]{2,1,0:T(2,128)(2,1)S(1)}, bf16[12,2,128]{2,1,0:T(2,128)(2,1)S(1)}, u32[]{:S(2)}, u32[]{:S(2)}) collective-permute-start(bf16[12,2,128]{2,1,0:T(2,128)(2,1)S(1)} %get-tuple-element.33), channel_id=1, source_target_pairs={{2,0},{3,1},{6,4},{7,5},{10,8},{11,9},{14,12},{15,13},{18,16},{19,... | collective-permute-start | bytes 18440 | tf_op jit(solution)/shard_map/ppermute | solution.py:17
  94.6 1.0 copy-start.2
  94.7 2.0 %copy-start.1 = (bf16[1300,128]{1,0:T(8,128)(2,1)S(1)}, bf16[1300,128]{1,0:T(8,128)(2,1)}, u32[]{:S(2)}) copy-start(bf16[1300,128]{1,0:T(8,128)(2,1)} %reshape.257) | copy-start | bytes 998404
  95.6 2.3 %copy-start.4 = (bf16[1300,128]{1,0:T(8,128)(2,1)S(1)}, bf16[1300,128]{1,0:T(8,128)(2,1)}, u32[]{:S(2)}) copy-start(bf16[1300,128]{1,0:T(8,128)(2,1)} %reshape.259) | copy-start | bytes 998404
  96.7 2.3 %copy-start.3 = (bf16[1300,128]{1,0:T(8,128)(2,1)S(1)}, bf16[1300,128]{1,0:T(8,128)(2,1)}, u32[]{:S(2)}) copy-start(bf16[1300,128]{1,0:T(8,128)(2,1)} %reshape.260) | copy-start | bytes 998404
  96.7 2.3 %copy-start.10 = (bf16[3,3,128,128]{3,2,1,0:T(8,128)(2,1)S(1)}, bf16[3,3,128,128]{3,2,1,0:T(8,128)(2,1)}, u32[]{:S(2)}) copy-start(bf16[3,3,128,128]{3,2,1,0:T(8,128)(2,1)} %param.16) | copy-start | bytes 884740
  100.6 0.7 copy-start.11
  101.5 1.0 copy-start.9
  103.5 0.7 copy-start.12
  103.5 0.7 copy-start.13
where the time goes:
time: 106 us; the launch traced here: 105 us
  starting transfers between devices  27.8 us (26%)
  between operations  24.6 us (23%)
  local copies, waits for them, and re-layouts  21.4 us (20%)
  waiting for transfers between devices  15.8 us (15%)
  matrix products  10.9 us (10%)
  other arithmetic  4.83 us (5%)
    ppermute x6, starting transfers between devices, extended(): before = lax.ppermute(last, axis, up)  15.8 us
    ppermute x6, starting transfers between devices, extended(): after = lax.ppermute(first, axis, down)  11.9 us
    ppermute x6, waiting for transfers between devices, extended(): after = lax.ppermute(first, axis, down)  11.5 us
    dot_general x26, matrix products, conv_three(): jnp.dot(window, weights[row_tap, col_tap], preferred_element_type=jnp.flo...  9.4 us
    dynamic_update_slice x9, local copies, waits for them, and re-layouts, regrid(): lax.dynamic_update_slice(counts, region_count + present, (top, left))  5.36 us
    dynamic_update_slice x9, local copies, waits for them, and re-layouts, regrid(): canvas = lax.dynamic_update_slice(canvas, region + piece, (top, left, zero))  4.46 us
    ppermute x6, waiting for transfers between devices, extended(): before = lax.ppermute(last, axis, up)  4.33 us
    reshape x9, local copies, waits for them, and re-layouts, conv_three(): padded[row_tap:row_tap + out_rows, col_tap:col_tap + out_cols]  3.69 us
  transfers between devices with their start and end apart: 13, of which 7 were waited for; matrix products, arithmetic and copies ran while one was open for 12% of the time, Pallas kernels for 0%

commit v1 on v0

v1 whole, which is shorter than its diff:
```python
import functools

import jax
import jax.numpy as jnp
from jax import lax
from jax.experimental import pallas as pl
from jax.experimental.pallas import tpu as pltpu
from jax.sharding import PartitionSpec as P

MO = 4
HALO = (3, 2 + MO + 1)
SIDE = 16
MESH = pl.DeviceIdType.MESH
F32 = jnp.float32
BF16 = jnp.bfloat16


def kernel(
    sizes,
    feat,
    shift_ref,
    w_lat,
    b_lat,
    w_fpn,
    w_dec1,
    b_dec1,
    w_dec2,
    b_dec2,
    w_out,
    b_out,
    out_ref,
    field,
    lat6,
    pyr_a,
    pyr_b,
    dif6,
    hid6,
    wl2,
    wf2,
    wd1,
    wd2,
    send_sem,
    recv_sem,
    copy_sem,
):
    row_tiles, col_tiles, tile_rows, tile_cols = sizes
    half = tile_rows // 2
    wide = tile_cols + 2 * SIDE
    mid = tile_cols + SIDE
    rows_of = tuple(half + 2 * h for h in HALO)
    base_of = (0, rows_of[0])
    ch = feat.shape[2]
    r = lax.axis_index("rows")
    c = lax.axis_index("cols")
    d = lax.axis_index("date")
    upper = d == 0
    has_col = {0: c >= 0, 1: c + 1 < col_tiles, -1: c >= 1}
    has_down = r + 1 < row_tiles
    has_up = r >= 1
    other_row = jnp.where(upper, r - 1, r + 1)
    has_other = (other_row >= 0) & (other_row < row_tiles)

    def local(src, dst, index):
        copy = pltpu.make_async_copy(src, dst, copy_sem.at[index])
        copy.start()
        return copy

    depth = 9 * ch
    lat_copies = [
        local(w_lat, wl2.at[pl.ds(0, ch), pl.ds(0, ch)], 0),
        local(w_lat, wl2.at[pl.ds(ch, ch), pl.ds(ch, ch)], 1),
    ]
    conv_copies = []
    for at, (src, dst) in enumerate(((w_fpn, wf2), (w_dec1, wd1), (w_dec2, wd2))):
        conv_copies.append(
            (
                local(src, dst.at[pl.ds(0, depth), pl.ds(0, ch)], 2 + 2 * at),
                local(src, dst.at[pl.ds(3 * ch, depth), pl.ds(ch, ch)], 3 + 2 * at),
            )
        )

    barrier = pltpu.get_barrier_semaphore()
    for step in (0, 1, -1):
        for date in (0, 1):
            here = has_col[step] if step else d != date

            @pl.when(here)
            def _():
                pl.semaphore_signal(
                    barrier,
                    inc=1,
                    device_id={"rows": r, "cols": c + step, "date": date},
                    device_id_type=MESH,
                )

            @pl.when(has_col[step] & has_other)
            def _():
                pl.semaphore_signal(
                    barrier,
                    inc=1,
                    device_id={"rows": other_row, "cols": c + step, "date": date},
                    device_id_type=MESH,
                )

    wl2[0:ch, ch:] = jnp.zeros((ch, ch), BF16)
    wl2[ch:, 0:ch] = jnp.zeros((ch, ch), BF16)
    for dst in (wf2, wd1, wd2):
        dst[depth:, 0:ch] = jnp.zeros((3 * ch, ch), BF16)
        dst[0 : 3 * ch, ch:] = jnp.zeros((3 * ch, ch), BF16)

    def start_row(date, place, kind):
        own = HALO[date] if place == 0 else 0
        other = 0 if place == 0 else half + HALO[date]
        return base_of[date] + (own if kind == 0 else other)

    for place in (0, 1):

        @pl.when((d == place) & jnp.logical_not(has_other))
        def _():
            for date in (0, 1):
                first = start_row(date, place, 1)
                field[first : first + HALO[date]] = jnp.zeros((HALO[date], wide, ch), BF16)

    cols_beside = jnp.where(has_col[1], 1, 0) + jnp.where(has_col[-1], 1, 0) + 1
    rows_beside = jnp.where(has_down, 1, 0) + jnp.where(has_up, 1, 0)
    pl.semaphore_wait(barrier, (2 + rows_beside) * cols_beside - 1)

    def pieces(date):
        h = HALO[date]
        found = []
        for rk, (row_step, place, ok) in enumerate(
            (
                (0, 1 - date, None),
                (0, date, None),
                (1, 0, has_down),
                (-1, 1, has_up),
            )
        ):
            kind = 0 if row_step == 0 else 1
            count = half + h if kind == 0 else h
            if kind == 0:
                src_row = 0 if place == 0 else half - h
            else:
                src_row = tile_rows - h if place == 0 else 0
            dst_row = start_row(date, place, kind)
            for ck, step in enumerate((0, 1, -1)):
                if rk == 1 and step == 0:
                    continue
                src_col, dst_col, width = (
                    (0, SIDE, tile_cols),
                    (tile_cols - SIDE, 0, SIDE),
                    (0, SIDE + tile_cols, SIDE),
                )[ck]
                go = has_col[step]
                if ok is not None:
                    go = go & ok
                copy = pltpu.make_async_remote_copy(
                    src_ref=feat.at[pl.ds(src_row, count), pl.ds(src_col, width)],
                    dst_ref=field.at[pl.ds(dst_row, count), pl.ds(dst_col, width)],
                    send_sem=send_sem.at[rk, ck],
                    recv_sem=recv_sem.at[date, kind, ck],
                    device_id={"rows": r + row_step, "cols": c + step, "date": place},
                    device_id_type=MESH,
                )
                found.append(((kind, -abs(step)), go, copy))
        found.sort(key=lambda item: item[0])
        return [item[1:] for item in found]

    def own_copy(date):
        h = HALO[date]
        return pltpu.make_async_copy(
            feat.at[pl.ds(0 if date == 0 else half - h, half + h)],
            field.at[pl.ds(start_row(date, date, 0), half + h), pl.ds(SIDE, tile_cols)],
            recv_sem.at[date, 0, 0],
        )

    for date in (0, 1):

        @pl.when(d == date)
        def _():
            for go, copy in pieces(date):

                @pl.when(go)
                def _():
                    copy.start()

            own_copy(date).start()

    def await_kind(kind):
        for date in (0, 1):
            h = HALO[date]
            count = half + h if kind == 0 else h
            first = jnp.where(upper, start_row(date, 0, kind), start_row(date, 1, kind))
            for ck, step in enumerate((0, -1, 1)):
                dst_col, width = ((SIDE, tile_cols), (0, SIDE), (SIDE + tile_cols, SIDE))[ck]
                view = field.at[pl.ds(first, count), pl.ds(dst_col, width)]

                def wait():
                    pltpu.make_async_copy(view, view, recv_sem.at[date, kind, ck]).wait()

                ok = has_col[step]
                if kind == 1:
                    ok = ok & has_other
                pl.when(ok)(wait)

    far = 1 << 20
    origin = (2 * r + d) * half
    rows_total = row_tiles * tile_rows
    left_end = -c * tile_cols
    right_end = (col_tiles - c) * tile_cols
    x_wide = lax.broadcasted_iota(jnp.int32, (wide, ch), 0) - SIDE
    x_mid = lax.broadcasted_iota(jnp.int32, (mid, ch), 0) - SIDE // 2
    edge = SIDE // 2

    def inside(x, y):
        row = origin + y
        end = jnp.where((row >= 0) & (row < rows_total), right_end, -far)
        return (x >= left_end) & (x < end)

    def put_taps(dst, pair, slot, value, lo, hi):
        total = value.shape[0]
        at = slot * 3 * ch
        taps = (pltpu.roll(value, 1, 0), value, pltpu.roll(value, total - 1, 0))
        for tap, moved in enumerate(taps):
            dst[pair, :, at + tap * ch : at + (tap + 1) * ch] = moved[lo:hi].astype(BF16)

    lat_bias = b_lat[...]

    def lateral_pair(date, q):
        first = base_of[date] + 2 * q
        both = jnp.concatenate([field[first], field[first + 1]], axis=-1)
        value = jnp.dot(both, wl2[...], preferred_element_type=F32)
        for slot in (0, 1):
            y = 2 * q + slot - HALO[date]
            part = value[:, slot * ch : (slot + 1) * ch] + lat_bias
            part = jnp.where(inside(x_wide, y), part, 0.0)
            put_taps(lat6, base_of[date] // 2 + q, slot, part, edge, wide - edge)

    def conv_pairs(src, weights, first, count):
        width, deep = src.shape[1:]
        top = src[pl.ds(first, count)].reshape(count * width, deep)
        low = src[pl.ds(first + 1, count)].reshape(count * width, deep)
        return jnp.dot(top, weights[0:deep], preferred_element_type=F32) + jnp.dot(
            low, weights[deep:], preferred_element_type=F32
        )

    def pyramid_pairs(date, q, count):
        value = conv_pairs(lat6, wf2, base_of[date] // 2 + q, count)
        value = value.astype(BF16).astype(F32)
        for pair in range(count):
            for slot in (0, 1):
                part = value[pair * mid : (pair + 1) * mid, slot * ch : (slot + 1) * ch]
                if date == 0:
                    pyr_a[2 * (q + pair) + slot] = part
                else:
                    pyr_b[2 * (q + pair) + slot, edge : edge + mid] = part

    def phase(kind):
        for date in (0, 1):
            pairs = rows_of[date] // 2
            late = (HALO[date] + 1) // 2
            count = pairs - late if kind == 0 else late
            low_first = 0 if kind == 0 else pairs - late
            first = jnp.where(upper, pairs - count - low_first, low_first)

            def body(i, carry):
                lateral_pair(date, first + i)
                return carry

            lax.fori_loop(0, count, body, 0)
        if kind == 0:
            for copy in conv_copies[0]:
                copy.wait()
        for date in (0, 1):
            pairs = rows_of[date] // 2 - 1
            late = (HALO[date] + 1) // 2
            count = pairs - late if kind == 0 else late
            low_first = 0 if kind == 0 else pairs - late
            first = jnp.where(upper, pairs - count - low_first, low_first)

            def body(i, carry):
                pyramid_pairs(date, first + 2 * i, 2)
                return carry

            lax.fori_loop(0, count // 2, body, 0)

    for copy in lat_copies:
        copy.wait()
    await_kind(0)
    phase(0)
    await_kind(1)
    phase(1)

    tiles = []
    for kind in (0, 1):
        tile_row = r if kind == 0 else jnp.clip(other_row, 0, row_tiles - 1)
        for step in (0, -1, 1):
            tile = tile_row * col_tiles + jnp.clip(c + step, 0, col_tiles - 1)
            ok = has_col[step]
            if kind == 1:
                ok = ok & has_other
            tiles.append((kind, step, ok, shift_ref[2 * tile], shift_ref[2 * tile + 1]))
    reach = HALO[1] - 1
    x_left = x_mid[0:SIDE]
    x_right = x_mid[mid - SIDE : mid]

    def regrid_row(p, slot):
        y = 2 * p + slot - 2
        sums = {0: 0.0, -1: 0.0, 1: 0.0}
        seen = {0: 0.0, -1: 0.0, 1: 0.0}
        for kind, step, ok, row_by, col_by in tiles:
            u = y + d * half - row_by
            within = (u >= 0) & (u < tile_rows)
            use = ok & (within if kind == 0 else jnp.logical_not(within))
            if step == 0:
                x, start, size = x_mid, 0, mid
                low, high = col_by, tile_cols + col_by
            elif step == -1:
                x, start, size = x_left, 0, SIDE
                low, high = -far, col_by
            else:
                x, start, size = x_right, mid - SIDE, SIDE
                low, high = tile_cols + col_by, far
            mask = (x >= low) & (x < jnp.where(use, high, -2 * far))
            piece = pyr_b[y - row_by + reach, pl.ds(start + edge - col_by, size), :]
            sums[step] = sums[step] + jnp.where(mask, piece, 0.0)
            seen[step] = seen[step] + jnp.where(mask, 1.0, 0.0)

        def whole(parts):
            full = parts[0]
            return jnp.concatenate(
                [
                    full[0:SIDE] + parts[-1],
                    full[SIDE : mid - SIDE],
                    full[mid - SIDE :] + parts[1],
                ],
                axis=0,
            )

        total, cover = whole(sums), whole(seen)
        placed = total / jnp.maximum(cover, 1.0)
        diff = jnp.abs(pyr_a[2 * p + slot] - placed) * jnp.minimum(cover, 1.0)
        diff = jnp.where(inside(x_mid, y), diff, 0.0)
        put_taps(dif6, p, slot, diff, 0, mid)

    def regrid_body(p, carry):
        regrid_row(p, 0)
        regrid_row(p, 1)
        return carry

    lax.fori_loop(0, half // 2 + 2, regrid_body, 0)

    for copy in conv_copies[1]:
        copy.wait()
    bias_one = b_dec1[...]

    def dec_one(i, carry):
        value = conv_pairs(dif6, wd1, i, 1)
        for slot in (0, 1):
            part = jnp.maximum(value[:, slot * ch : (slot + 1) * ch] + bias_one, 0.0)
            part = jnp.where(inside(x_mid, 2 * i + slot - 1), part, 0.0)
            put_taps(hid6, i, slot, part, edge, mid - edge)
        return carry

    lax.fori_loop(0, half // 2 + 1, dec_one, 0)

    for copy in conv_copies[2]:
        copy.wait()
    bias_two = b_dec2[...]
    out_w = jnp.broadcast_to(w_out[...].astype(F32), (16, ch)).astype(BF16)
    out_b = b_out[0]
    for i in range(0, half // 2, 2):
        value = conv_pairs(hid6, wd2, i, 2)
        for pair in (0, 1):
            for slot in (0, 1):
                part = value[pair * tile_cols : (pair + 1) * tile_cols, slot * ch : (slot + 1) * ch]
                part = jnp.maximum(part + bias_two, 0.0).astype(BF16)
                logit = lax.dot_general(
                    out_w, part, (((1,), (1,)), ((), ())), preferred_element_type=F32
                )
                y = 2 * (i + pair) + slot
                out_ref[y : y + 1, :] = logit[0:1] + out_b

    for date in (0, 1):

        @pl.when(d == date)
        def _():
            for go, copy in pieces(date):

                @pl.when(go)
                def _():
                    copy.wait_send()


def per_device(
    features, scene_shift, w_lat, b_lat, w_fpn, w_dec1, b_dec1, w_dec2, b_dec2, w_out, b_out
):
    tile_rows, tile_cols, ch = features.shape[1:]
    half = tile_rows // 2
    sizes = (lax.axis_size("rows"), lax.axis_size("cols"), tile_rows, tile_cols)
    rows_of = tuple(half + 2 * h for h in HALO)
    wide, mid = tile_cols + 2 * SIDE, tile_cols + SIDE
    any_spec = pl.BlockSpec(memory_space=pl.ANY)
    vmem = pl.BlockSpec(memory_space=pltpu.VMEM)
    smem = pl.BlockSpec(memory_space=pltpu.SMEM)
    flops = 2 * ch * ch * tile_cols * 9 * 60
    return pl.pallas_call(
        functools.partial(kernel, sizes),
        out_shape=jax.ShapeDtypeStruct((half, tile_cols), F32),
        in_specs=[
            any_spec,
            smem,
            any_spec,
            vmem,
            any_spec,
            any_spec,
            vmem,
            any_spec,
            vmem,
            vmem,
            smem,
        ],
        out_specs=vmem,
        scratch_shapes=[
            pltpu.VMEM((sum(rows_of), wide, ch), BF16),
            pltpu.VMEM((sum(rows_of) // 2, mid, 6 * ch), BF16),
            pltpu.VMEM((half + 4, mid, ch), F32),
            pltpu.VMEM((half + 2 * HALO[1] - 2, wide, ch), F32),
            pltpu.VMEM((half // 2 + 2, mid, 6 * ch), BF16),
            pltpu.VMEM((half // 2 + 1, tile_cols, 6 * ch), BF16),
            pltpu.VMEM((2 * ch, 2 * ch), BF16),
            pltpu.VMEM((12 * ch, 2 * ch), BF16),
            pltpu.VMEM((12 * ch, 2 * ch), BF16),
            pltpu.VMEM((12 * ch, 2 * ch), BF16),
            pltpu.SemaphoreType.DMA((4, 3)),
            pltpu.SemaphoreType.DMA((2, 2, 3)),
            pltpu.SemaphoreType.DMA((8,)),
        ],
        compiler_params=pltpu.CompilerParams(
            collective_id=0, has_side_effects=True, vmem_limit_bytes=48 << 20
        ),
        cost_estimate=pl.CostEstimate(flops=flops, bytes_accessed=4 << 20, transcendentals=0),
    )(
        features[0],
        scene_shift.reshape(-1),
        w_lat,
        b_lat.reshape(1, ch),
        w_fpn.reshape(9 * ch, ch),
        w_dec1.reshape(9 * ch, ch),
        b_dec1.reshape(1, ch),
        w_dec2.reshape(9 * ch, ch),
        b_dec2.reshape(1, ch),
        w_out.reshape(1, ch),
        b_out,
    )


def solution(mesh):
    return jax.shard_map(
        per_device,
        mesh=mesh,
        in_specs=(
            P("date", ("groups", "rows"), "cols", None),
            P("groups", None, None),
            P(),
            P(),
            P(),
            P(),
            P(),
            P(),
            P(),
            P(),
            P(),
        ),
        out_specs=P(("groups", "rows", "date"), "cols"),
        check_vma=False,
    )
```

time: 106 us -> 28.4 us (0.27)
  the two profiles are of different devices: /device:TPU:12 before, /device:TPU:0 now
where the time goes in v1:
time: 28.4 us; the launch traced here: 28 us
  Pallas kernels  20.6 us (73%)
  local copies, waits for them, and re-layouts  6.74 us (24%)
  between operations  0.68 us (2%)
    pallas_call x1, Pallas kernels, per_device(): pl.pallas_call(functools.partial(kernel, sizes), out_shape=jax.ShapeDtype...  20.6 us
    unnamed x22, local copies, waits for them, and re-layouts  6.66 us

profile of v1, /device:TPU:0, one launch (start us, length us, event | category | flops | bytes accessed | tf_op | source)
XLA Modules:
  0.0 28.0 jit_solution(3806343635524109303)
XLA Ops:
  0.7 0.0 copy-start.9
  0.7 0.7 %copy-done.9 = s32[4,2,2]{0,2,1:T(2,128)S(1)} copy-done((s32[4,2,2]{0,2,1:T(2,128)S(1)}, s32[4,2,2]{0,2,1:T(2,128)}, u32[]{:S(2)}) %copy-start.9) | copy-done | bytes 88
  1.3 0.1 copy.13
  1.4 0.0 copy-start.5
  1.4 0.0 copy-start.6
  1.4 0.0 copy-start.7
  1.4 0.0 copy-start.8
  1.4 0.1 reshape.24.shift_ref
  1.5 0.6 %copy-done.5 = f32[128]{0:T(128)S(1)} copy-done((f32[128]{0:T(128)S(1)}, f32[128]{0:T(128)}, u32[]{:S(2)}) %copy-start.5) | copy-done | bytes 536
  2.1 0.0 copy-done.6
  2.1 0.0 copy-done.7
  2.1 0.0 copy-done.8
  2.1 0.0 copy-start
  2.1 1.0 %copy-done = bf16[1,16,128,128]{3,2,1,0:T(8,128)(2,1)S(1)} copy-done((bf16[1,16,128,128]{3,2,1,0:T(8,128)(2,1)S(1)}, bf16[1,16,128,128]{3,2,1,0:T(8,128)(2,1)}, u32[]{:S(2)}) %copy-start) | copy-done | bytes 524312
  3.2 0.0 copy-start.1
  3.2 1.0 %copy-done.1 = bf16[3,3,128,128]{3,2,1,0:T(8,128)(2,1)S(1)} copy-done((bf16[3,3,128,128]{3,2,1,0:T(8,128)(2,1)S(1)}, bf16[3,3,128,128]{3,2,1,0:T(8,128)(2,1)}, u32[]{:S(2)}) %copy-start.1) | copy-done | bytes 294936
  4.1 0.0 copy-start.2
  4.1 1.0 %copy-done.2 = bf16[3,3,128,128]{3,2,1,0:T(8,128)(2,1)S(1)} copy-done((bf16[3,3,128,128]{3,2,1,0:T(8,128)(2,1)S(1)}, bf16[3,3,128,128]{3,2,1,0:T(8,128)(2,1)}, u32[]{:S(2)}) %copy-start.2) | copy-done | bytes 294936
  5.1 0.0 copy-start.3
  5.1 1.0 %copy-done.3 = bf16[3,3,128,128]{3,2,1,0:T(8,128)(2,1)S(1)} copy-done((bf16[3,3,128,128]{3,2,1,0:T(8,128)(2,1)S(1)}, bf16[3,3,128,128]{3,2,1,0:T(8,128)(2,1)}, u32[]{:S(2)}) %copy-start.3) | copy-done | bytes 294936
  6.1 0.0 copy-start.4
  6.1 0.8 %copy-done.4 = bf16[128,128]{1,0:T(8,128)(2,1)S(1)} copy-done((bf16[128,128]{1,0:T(8,128)(2,1)S(1)}, bf16[128,128]{1,0:T(8,128)(2,1)}, u32[]{:S(2)}) %copy-start.4) | copy-done | bytes 32792
  6.8 20.6 %shard_map.109 = f32[8,128]{1,0:T(8,128)S(1)} custom-call(bf16[16,128,128]{2,1,0:T(8,128)(2,1)S(1)} %bitcast.8, s32[16]{0:T(128)S(1)} %reshape.24.shift_ref, bf16[128,128]{1,0:T(8,128)(2,1)S(1)} %copy-done.4, f32[1,128]{1,0:T(1,128)S(1)} %bitcast.12, bf16[1152,128]{1,0:T(8,128)(2,1)S(1)} %bitcast.9, bf16[1152,128]{1,0:T(8,128)(2,1)S(1)} %bitcast.10, ...), custom_call_target="tpu_custom_call" | custom-call | flops 2264924160 | bytes 4194304 | tf_op jit(solution)/shard_map/pallas_call | solution.py:407
  27.4 0.6 %copy.16 = f32[8,128]{1,0:T(8,128)} copy(f32[8,128]{1,0:T(8,128)S(1)} %shard_map.109) | data formatting | bytes 8192
Async XLA Ops:
  0.7 0.7 %copy-start.9 = (s32[4,2,2]{0,2,1:T(2,128)S(1)}, s32[4,2,2]{0,2,1:T(2,128)}, u32[]{:S(2)}) copy-start(s32[4,2,2]{0,2,1:T(2,128)} %param.12) | copy-start | bytes 196
  1.4 0.7 %copy-start.5 = (f32[128]{0:T(128)S(1)}, f32[128]{0:T(128)}, u32[]{:S(2)}) copy-start(f32[128]{0:T(128)} %param.14) | copy-start | bytes 1540
  1.4 0.7 %copy-start.6 = (f32[128]{0:T(128)S(1)}, f32[128]{0:T(128)}, u32[]{:S(2)}) copy-start(f32[128]{0:T(128)} %param.17) | copy-start | bytes 1540
  1.4 0.7 %copy-start.7 = (f32[128]{0:T(128)S(1)}, f32[128]{0:T(128)}, u32[]{:S(2)}) copy-start(f32[128]{0:T(128)} %param.19) | copy-start | bytes 1540
  1.4 0.7 %copy-start.8 = (bf16[128]{0:T(256)(128)(2,1)S(1)}, bf16[128]{0:T(256)(128)(2,1)}, u32[]{:S(2)}) copy-start(bf16[128]{0:T(256)(128)(2,1)} %param.20) | copy-start | bytes 772
  2.1 1.0 %copy-start = (bf16[1,16,128,128]{3,2,1,0:T(8,128)(2,1)S(1)}, bf16[1,16,128,128]{3,2,1,0:T(8,128)(2,1)}, u32[]{:S(2)}) copy-start(bf16[1,16,128,128]{3,2,1,0:T(8,128)(2,1)} %param.11) | copy-start | bytes 1572868
  3.2 1.0 %copy-start.1 = (bf16[3,3,128,128]{3,2,1,0:T(8,128)(2,1)S(1)}, bf16[3,3,128,128]{3,2,1,0:T(8,128)(2,1)}, u32[]{:S(2)}) copy-start(bf16[3,3,128,128]{3,2,1,0:T(8,128)(2,1)} %param.15) | copy-start | bytes 884740
  4.1 1.0 %copy-start.2 = (bf16[3,3,128,128]{3,2,1,0:T(8,128)(2,1)S(1)}, bf16[3,3,128,128]{3,2,1,0:T(8,128)(2,1)}, u32[]{:S(2)}) copy-start(bf16[3,3,128,128]{3,2,1,0:T(8,128)(2,1)} %param.16) | copy-start | bytes 884740
  5.1 1.0 %copy-start.3 = (bf16[3,3,128,128]{3,2,1,0:T(8,128)(2,1)S(1)}, bf16[3,3,128,128]{3,2,1,0:T(8,128)(2,1)}, u32[]{:S(2)}) copy-start(bf16[3,3,128,128]{3,2,1,0:T(8,128)(2,1)} %param.18) | copy-start | bytes 884740
  6.1 0.8 %copy-start.4 = (bf16[128,128]{1,0:T(8,128)(2,1)S(1)}, bf16[128,128]{1,0:T(8,128)(2,1)}, u32[]{:S(2)}) copy-start(bf16[128,128]{1,0:T(8,128)(2,1)} %w_lat.1) | copy-start | bytes 98308

commit v2 on v1

--- a/solution.py
+++ b/solution.py
@@ -9,7 +9,7 @@
 
 MO = 4
 HALO = (3, 2 + MO + 1)
-SIDE = 16
+SIDE = 8
 MESH = pl.DeviceIdType.MESH
 F32 = jnp.float32
 BF16 = jnp.bfloat16
@@ -39,17 +39,22 @@
     wf2,
     wd1,
     wd2,
+    vec_lat,
+    vec_one,
+    vec_two,
+    vec_out,
     send_sem,
     recv_sem,
     copy_sem,
 ):
     row_tiles, col_tiles, tile_rows, tile_cols = sizes
     half = tile_rows // 2
-    wide = tile_cols + 2 * SIDE
-    mid = tile_cols + SIDE
+    mid = tile_cols + 2 * SIDE
+    groups = mid // SIDE
+    core = tile_cols // SIDE
     rows_of = tuple(half + 2 * h for h in HALO)
     base_of = (0, rows_of[0])
-    ch = feat.shape[2]
+    ch = feat.shape[3]
     r = lax.axis_index("rows")
     c = lax.axis_index("cols")
     d = lax.axis_index("date")
@@ -70,14 +75,18 @@
         local(w_lat, wl2.at[pl.ds(0, ch), pl.ds(0, ch)], 0),
         local(w_lat, wl2.at[pl.ds(ch, ch), pl.ds(ch, ch)], 1),
     ]
+    lat_copies.append(local(b_lat, vec_lat, 8))
     conv_copies = []
     for at, (src, dst) in enumerate(((w_fpn, wf2), (w_dec1, wd1), (w_dec2, wd2))):
         conv_copies.append(
-            (
+            [
                 local(src, dst.at[pl.ds(0, depth), pl.ds(0, ch)], 2 + 2 * at),
                 local(src, dst.at[pl.ds(3 * ch, depth), pl.ds(ch, ch)], 3 + 2 * at),
-            )
+            ]
         )
+    conv_copies[1].append(local(b_dec1, vec_one, 9))
+    conv_copies[2].append(local(b_dec2, vec_two, 10))
+    conv_copies[2].append(local(w_out, vec_out, 11))
 
     barrier = pltpu.get_barrier_semaphore()
     for step in (0, 1, -1):
@@ -119,7 +128,7 @@
         def _():
             for date in (0, 1):
                 first = start_row(date, place, 1)
-                field[first : first + HALO[date]] = jnp.zeros((HALO[date], wide, ch), BF16)
+                field[first : first + HALO[date]] = jnp.zeros((HALO[date], groups, SIDE, ch), BF16)
 
     cols_beside = jnp.where(has_col[1], 1, 0) + jnp.where(has_col[-1], 1, 0) + 1
     rows_beside = jnp.where(has_down, 1, 0) + jnp.where(has_up, 1, 0)
@@ -147,9 +156,9 @@
                 if rk == 1 and step == 0:
                     continue
                 src_col, dst_col, width = (
-                    (0, SIDE, tile_cols),
-                    (tile_cols - SIDE, 0, SIDE),
-                    (0, SIDE + tile_cols, SIDE),
+                    (0, 1, core),
+                    (core - 1, 0, 1),
+                    (0, 1 + core, 1),
                 )[ck]
                 go = has_col[step]
                 if ok is not None:
@@ -170,7 +179,7 @@
         h = HALO[date]
         return pltpu.make_async_copy(
             feat.at[pl.ds(0 if date == 0 else half - h, half + h)],
-            field.at[pl.ds(start_row(date, date, 0), half + h), pl.ds(SIDE, tile_cols)],
+            field.at[pl.ds(start_row(date, date, 0), half + h), pl.ds(1, core)],
             recv_sem.at[date, 0, 0],
         )
 
@@ -192,7 +201,7 @@
             count = half + h if kind == 0 else h
             first = jnp.where(upper, start_row(date, 0, kind), start_row(date, 1, kind))
             for ck, step in enumerate((0, -1, 1)):
-                dst_col, width = ((SIDE, tile_cols), (0, SIDE), (SIDE + tile_cols, SIDE))[ck]
+                dst_col, width = ((1, core), (0, 1), (1 + core, 1))[ck]
                 view = field.at[pl.ds(first, count), pl.ds(dst_col, width)]
 
                 def wait():
@@ -208,9 +217,8 @@
     rows_total = row_tiles * tile_rows
     left_end = -c * tile_cols
     right_end = (col_tiles - c) * tile_cols
-    x_wide = lax.broadcasted_iota(jnp.int32, (wide, ch), 0) - SIDE
-    x_mid = lax.broadcasted_iota(jnp.int32, (mid, ch), 0) - SIDE // 2
-    edge = SIDE // 2
+    x_mid = lax.broadcasted_iota(jnp.int32, (mid, ch), 0) - SIDE
+    edge = SIDE
 
     def inside(x, y):
         row = origin + y
@@ -224,17 +232,17 @@
         for tap, moved in enumerate(taps):
             dst[pair, :, at + tap * ch : at + (tap + 1) * ch] = moved[lo:hi].astype(BF16)
 
-    lat_bias = b_lat[...]
-
     def lateral_pair(date, q):
         first = base_of[date] + 2 * q
-        both = jnp.concatenate([field[first], field[first + 1]], axis=-1)
+        both = jnp.concatenate(
+            [field[first + slot].reshape(mid, ch) for slot in (0, 1)], axis=-1
+        )
         value = jnp.dot(both, wl2[...], preferred_element_type=F32)
         for slot in (0, 1):
             y = 2 * q + slot - HALO[date]
             part = value[:, slot * ch : (slot + 1) * ch] + lat_bias
-            part = jnp.where(inside(x_wide, y), part, 0.0)
-            put_taps(lat6, base_of[date] // 2 + q, slot, part, edge, wide - edge)
+            part = jnp.where(inside(x_mid, y), part, 0.0)
+            put_taps(lat6, base_of[date] // 2 + q, slot, part, 0, mid)
 
     def conv_pairs(src, weights, first, count):
         width, deep = src.shape[1:]
@@ -267,7 +275,7 @@
                 lateral_pair(date, first + i)
                 return carry
 
-            lax.fori_loop(0, count, body, 0)
+            lax.fori_loop(0, count, body, 0, unroll=True)
         if kind == 0:
             for copy in conv_copies[0]:
                 copy.wait()
@@ -282,10 +290,11 @@
                 pyramid_pairs(date, first + 2 * i, 2)
                 return carry
 
-            lax.fori_loop(0, count // 2, body, 0)
+            pyramid_pairs(date, first, count)
 
     for copy in lat_copies:
         copy.wait()
+    lat_bias = vec_lat[...]
     await_kind(0)
     phase(0)
     await_kind(1)
@@ -295,14 +304,14 @@
     for kind in (0, 1):
         tile_row = r if kind == 0 else jnp.clip(other_row, 0, row_tiles - 1)
         for step in (0, -1, 1):
-            tile = tile_row * col_tiles + jnp.clip(c + step, 0, col_tiles - 1)
+            tile_col = jnp.clip(c + step, 0, col_tiles - 1)
             ok = has_col[step]
             if kind == 1:
                 ok = ok & has_other
-            tiles.append((kind, step, ok, shift_ref[2 * tile], shift_ref[2 * tile + 1]))
+            tiles.append((kind, step, ok, shift_ref[tile_col, 0, tile_row], shift_ref[tile_col, 1, tile_row]))
     reach = HALO[1] - 1
-    x_left = x_mid[0:SIDE]
-    x_right = x_mid[mid - SIDE : mid]
+    x_left = x_mid[0 : 2 * SIDE]
+    x_right = x_mid[mid - 2 * SIDE : mid]
 
     def regrid_row(p, slot):
         y = 2 * p + slot - 2
@@ -316,10 +325,10 @@
                 x, start, size = x_mid, 0, mid
                 low, high = col_by, tile_cols + col_by
             elif step == -1:
-                x, start, size = x_left, 0, SIDE
+                x, start, size = x_left, 0, 2 * SIDE
                 low, high = -far, col_by
             else:
-                x, start, size = x_right, mid - SIDE, SIDE
+                x, start, size = x_right, mid - 2 * SIDE, 2 * SIDE
                 low, high = tile_cols + col_by, far
             mask = (x >= low) & (x < jnp.where(use, high, -2 * far))
             piece = pyr_b[y - row_by + reach, pl.ds(start + edge - col_by, size), :]
@@ -330,9 +339,9 @@
             full = parts[0]
             return jnp.concatenate(
                 [
-                    full[0:SIDE] + parts[-1],
-                    full[SIDE : mid - SIDE],
-                    full[mid - SIDE :] + parts[1],
+                    full[0 : 2 * SIDE] + parts[-1],
+                    full[2 * SIDE : mid - 2 * SIDE],
+                    full[mid - 2 * SIDE :] + parts[1],
                 ],
                 axis=0,
             )
@@ -352,26 +361,27 @@
 
     for copy in conv_copies[1]:
         copy.wait()
-    bias_one = b_dec1[...]
-
-    def dec_one(i, carry):
-        value = conv_pairs(dif6, wd1, i, 1)
-        for slot in (0, 1):
-            part = jnp.maximum(value[:, slot * ch : (slot + 1) * ch] + bias_one, 0.0)
-            part = jnp.where(inside(x_mid, 2 * i + slot - 1), part, 0.0)
-            put_taps(hid6, i, slot, part, edge, mid - edge)
-        return carry
-
-    lax.fori_loop(0, half // 2 + 1, dec_one, 0)
+    bias_one = vec_one[...]
+
+    def dec_one(i, count):
+        value = conv_pairs(dif6, wd1, i, count)
+        for pair in range(count):
+            for slot in (0, 1):
+                part = value[pair * mid : (pair + 1) * mid, slot * ch : (slot + 1) * ch]
+                part = jnp.maximum(part + bias_one, 0.0)
+                part = jnp.where(inside(x_mid, 2 * (i + pair) + slot - 1), part, 0.0)
+                put_taps(hid6, i + pair, slot, part, edge, mid - edge)
+
+    dec_one(0, half // 2 + 1)
 
     for copy in conv_copies[2]:
         copy.wait()
-    bias_two = b_dec2[...]
-    out_w = jnp.broadcast_to(w_out[...].astype(F32), (16, ch)).astype(BF16)
+    bias_two = vec_two[...]
+    out_w = jnp.broadcast_to(vec_out[...].astype(F32), (16, ch)).astype(BF16)
     out_b = b_out[0]
-    for i in range(0, half // 2, 2):
-        value = conv_pairs(hid6, wd2, i, 2)
-        for pair in (0, 1):
+    for i in range(0, half // 2, half // 2):
+        value = conv_pairs(hid6, wd2, i, half // 2)
+        for pair in range(half // 2):
             for slot in (0, 1):
                 part = value[pair * tile_cols : (pair + 1) * tile_cols, slot * ch : (slot + 1) * ch]
                 part = jnp.maximum(part + bias_two, 0.0).astype(BF16)
@@ -399,8 +409,8 @@
     half = tile_rows // 2
     sizes = (lax.axis_size("rows"), lax.axis_size("cols"), tile_rows, tile_cols)
     rows_of = tuple(half + 2 * h for h in HALO)
-    wide, mid = tile_cols + 2 * SIDE, tile_cols + SIDE
-    any_spec = pl.BlockSpec(memory_space=pl.ANY)
+    mid = tile_cols + 2 * SIDE
+    hbm = pl.BlockSpec(memory_space=pltpu.HBM)
     vmem = pl.BlockSpec(memory_space=pltpu.VMEM)
     smem = pl.BlockSpec(memory_space=pltpu.SMEM)
     flops = 2 * ch * ch * tile_cols * 9 * 60
@@ -408,41 +418,45 @@
         functools.partial(kernel, sizes),
         out_shape=jax.ShapeDtypeStruct((half, tile_cols), F32),
         in_specs=[
-            any_spec,
+            hbm,
             smem,
-            any_spec,
-            vmem,
-            any_spec,
-            any_spec,
-            vmem,
-            any_spec,
-            vmem,
-            vmem,
+            hbm,
+            hbm,
+            hbm,
+            hbm,
+            hbm,
+            hbm,
+            hbm,
+            hbm,
             smem,
         ],
         out_specs=vmem,
         scratch_shapes=[
-            pltpu.VMEM((sum(rows_of), wide, ch), BF16),
+            pltpu.VMEM((sum(rows_of), mid // SIDE, SIDE, ch), BF16),
             pltpu.VMEM((sum(rows_of) // 2, mid, 6 * ch), BF16),
             pltpu.VMEM((half + 4, mid, ch), F32),
-            pltpu.VMEM((half + 2 * HALO[1] - 2, wide, ch), F32),
+            pltpu.VMEM((half + 2 * HALO[1] - 2, mid + 2 * SIDE, ch), F32),
             pltpu.VMEM((half // 2 + 2, mid, 6 * ch), BF16),
             pltpu.VMEM((half // 2 + 1, tile_cols, 6 * ch), BF16),
             pltpu.VMEM((2 * ch, 2 * ch), BF16),
             pltpu.VMEM((12 * ch, 2 * ch), BF16),
             pltpu.VMEM((12 * ch, 2 * ch), BF16),
             pltpu.VMEM((12 * ch, 2 * ch), BF16),
+            pltpu.VMEM((1, ch), F32),
+            pltpu.VMEM((1, ch), F32),
+            pltpu.VMEM((1, ch), F32),
+            pltpu.VMEM((1, ch), BF16),
             pltpu.SemaphoreType.DMA((4, 3)),
             pltpu.SemaphoreType.DMA((2, 2, 3)),
-            pltpu.SemaphoreType.DMA((8,)),
+            pltpu.SemaphoreType.DMA((12,)),
         ],
         compiler_params=pltpu.CompilerParams(
-            collective_id=0, has_side_effects=True, vmem_limit_bytes=48 << 20
+            collective_id=0, has_side_effects=True, vmem_limit_bytes=60 << 20
         ),
         cost_estimate=pl.CostEstimate(flops=flops, bytes_accessed=4 << 20, transcendentals=0),
     )(
-        features[0],
-        scene_shift.reshape(-1),
+        features.reshape(tile_rows, tile_cols // SIDE, SIDE, ch),
+        scene_shift.transpose(1, 2, 0),
         w_lat,
         b_lat.reshape(1, ch),
         w_fpn.reshape(9 * ch, ch),

time: 28.4 us -> 19.1 us (0.67)
  the two profiles are of different devices: /device:TPU:0 before, /device:TPU:1 now
where the time goes in v2:
time: 19.1 us; the launch traced here: 18.9 us
  Pallas kernels  16.9 us (88%)
  local copies, waits for them, and re-layouts  1.28 us (7%)
  between operations  0.66 us (3%)
    pallas_call x1, Pallas kernels, per_device(): pl.pallas_call(functools.partial(kernel, sizes), out_shape=jax.ShapeDtype...  16.9 us
    unnamed x1, local copies, waits for them, and re-layouts  1.28 us

profile of v2, /device:TPU:1, one launch (start us, length us, event | category | flops | bytes accessed | tf_op | source)
XLA Modules:
  0.0 18.9 jit_solution(8903553207218114722)
XLA Ops:
  0.7 16.9 %shard_map.109 = f32[8,128]{1,0:T(8,128)} custom-call(bf16[16,16,8,128]{3,2,1,0:T(8,128)(2,1)} %bitcast.9, s32[2,2,4]{2,1,0:T(2,128)} %bitcast.13, bf16[128,128]{1,0:T(8,128)(2,1)} %w_lat.1, f32[1,128]{1,0:T(1,128)} %bitcast.14, bf16[1152,128]{1,0:T(8,128)(2,1)} %bitcast.10, bf16[1152,128]{1,0:T(8,128)(2,1)} %bitcast.11, f32[1,128]{1,0:T(1,128)} %bitcast.15, ...), custom_call_target="tpu_custom_call" | custom-call | flops 2264924160 | bytes 4194304 | tf_op jit(solution)/shard_map/pallas_call | solution.py:417
  17.6 1.3 %copy.14 = f32[8,128]{1,0:T(8,128)} copy(f32[8,128]{1,0:T(8,128)} %shard_map.109) | data formatting | bytes 8192

commit v3 on v2

--- a/solution.py
+++ b/solution.py
@@ -88,6 +88,25 @@
     conv_copies[2].append(local(b_dec2, vec_two, 10))
     conv_copies[2].append(local(w_out, vec_out, 11))
 
+    def start_row(date, place, kind):
+        own = HALO[date] if place == 0 else 0
+        other = 0 if place == 0 else half + HALO[date]
+        return base_of[date] + (own if kind == 0 else other)
+
+    def own_copy(date):
+        h = HALO[date]
+        return pltpu.make_async_copy(
+            feat.at[pl.ds(0 if date == 0 else half - h, half + h)],
+            field.at[pl.ds(start_row(date, date, 0), half + h), pl.ds(1, core)],
+            recv_sem.at[date, 0, 0],
+        )
+
+    for date in (0, 1):
+
+        @pl.when(d == date)
+        def _():
+            own_copy(date).start()
+
     barrier = pltpu.get_barrier_semaphore()
     for step in (0, 1, -1):
         for date in (0, 1):
@@ -116,11 +135,6 @@
     for dst in (wf2, wd1, wd2):
         dst[depth:, 0:ch] = jnp.zeros((3 * ch, ch), BF16)
         dst[0 : 3 * ch, ch:] = jnp.zeros((3 * ch, ch), BF16)
-
-    def start_row(date, place, kind):
-        own = HALO[date] if place == 0 else 0
-        other = 0 if place == 0 else half + HALO[date]
-        return base_of[date] + (own if kind == 0 else other)
 
     for place in (0, 1):
 
@@ -171,17 +185,10 @@
                     device_id={"rows": r + row_step, "cols": c + step, "date": place},
                     device_id_type=MESH,
                 )
-                found.append(((kind, -abs(step)), go, copy))
+                late = {(1, 0): 0, (0, 1): 1, (0, 0): 2, (1, 1): 3}[kind, abs(step)]
+                found.append((late, go, copy))
         found.sort(key=lambda item: item[0])
         return [item[1:] for item in found]
-
-    def own_copy(date):
-        h = HALO[date]
-        return pltpu.make_async_copy(
-            feat.at[pl.ds(0 if date == 0 else half - h, half + h)],
-            field.at[pl.ds(start_row(date, date, 0), half + h), pl.ds(1, core)],
-            recv_sem.at[date, 0, 0],
-        )
 
     for date in (0, 1):
 
@@ -193,15 +200,15 @@
                 def _():
                     copy.start()
 
-            own_copy(date).start()
-
-    def await_kind(kind):
-        for date in (0, 1):
+    def await_kind(kind, steps=(0, -1, 1), dates=(0, 1)):
+        for date in dates:
             h = HALO[date]
             count = half + h if kind == 0 else h
             first = jnp.where(upper, start_row(date, 0, kind), start_row(date, 1, kind))
             for ck, step in enumerate((0, -1, 1)):
                 dst_col, width = ((1, core), (0, 1), (1 + core, 1))[ck]
+                if step not in steps:
+                    continue
                 view = field.at[pl.ds(first, count), pl.ds(dst_col, width)]
 
                 def wait():
@@ -244,6 +251,48 @@
             part = jnp.where(inside(x_mid, y), part, 0.0)
             put_taps(lat6, base_of[date] // 2 + q, slot, part, 0, mid)
 
+    def pairs_first(date):
+        return jnp.where(upper, (HALO[date] + 1) // 2, 0)
+
+    def pairs_count(date):
+        return rows_of[date] // 2 - (HALO[date] + 1) // 2
+
+    def lateral_core(date):
+        none = jnp.zeros((SIDE, ch), F32)
+        for i in range(pairs_count(date)):
+            q = pairs_first(date) + i
+            first = base_of[date] + 2 * q
+            both = jnp.concatenate(
+                [field[first + slot, 1 : 1 + core].reshape(tile_cols, ch) for slot in (0, 1)],
+                axis=-1,
+            )
+            value = jnp.dot(both, wl2[...], preferred_element_type=F32)
+            for slot in (0, 1):
+                part = value[:, slot * ch : (slot + 1) * ch] + lat_bias
+                part = jnp.concatenate([none, part, none], axis=0)
+                put_taps(lat6, base_of[date] // 2 + q, slot, part, 0, mid)
+
+    def lateral_sides(date):
+        rows = 2 * pairs_count(date)
+        q = pairs_first(date)
+        strip = 3 * SIDE
+        for at, shift in ((0, 0), (groups - 3, SIDE)):
+            block = field[pl.ds(base_of[date] + 2 * q, rows), at : at + 3]
+            value = jnp.dot(
+                block.reshape(rows * strip, ch), wl2[0:ch, 0:ch], preferred_element_type=F32
+            )
+            x = lax.broadcasted_iota(jnp.int32, (rows, strip, ch), 1) + (at - 1) * SIDE
+            x = x.reshape(rows * strip, ch)
+            value = jnp.where((x >= left_end) & (x < right_end), value + lat_bias, 0.0)
+            taps = (pltpu.roll(value, 1, 0), value, pltpu.roll(value, rows * strip - 1, 0))
+            low = at * SIDE + shift
+            for i in range(rows):
+                pair = base_of[date] // 2 + q + i // 2
+                for tap, moved in enumerate(taps):
+                    lane = (i % 2) * 3 * ch + tap * ch
+                    part = moved[i * strip + shift : i * strip + shift + 2 * SIDE]
+                    lat6[pair, low : low + 2 * SIDE, lane : lane + ch] = part.astype(BF16)
+
     def conv_pairs(src, weights, first, count):
         width, deep = src.shape[1:]
         top = src[pl.ds(first, count)].reshape(count * width, deep)
@@ -264,7 +313,7 @@
                     pyr_b[2 * (q + pair) + slot, edge : edge + mid] = part
 
     def phase(kind):
-        for date in (0, 1):
+        for date in (0, 1) if kind == 1 else ():
             pairs = rows_of[date] // 2
             late = (HALO[date] + 1) // 2
             count = pairs - late if kind == 0 else late
@@ -295,7 +344,23 @@
     for copy in lat_copies:
         copy.wait()
     lat_bias = vec_lat[...]
-    await_kind(0)
+    for date in (0, 1):
+
+        @pl.when(d == date)
+        def _():
+            own_copy(date).wait()
+            lateral_core(date)
+
+    for date in (0, 1):
+
+        @pl.when(d != date)
+        def _():
+            await_kind(0, (0,), (date,))
+            lateral_core(date)
+
+    await_kind(0, (-1, 1))
+    for date in (0, 1):
+        lateral_sides(date)
     phase(0)
     await_kind(1)
     phase(1)
@@ -416,7 +481,7 @@
     flops = 2 * ch * ch * tile_cols * 9 * 60
     return pl.pallas_call(
         functools.partial(kernel, sizes),
-        out_shape=jax.ShapeDtypeStruct((half, tile_cols), F32),
+        out_shape=pltpu.VMEM((half, tile_cols), F32),
         in_specs=[
             hbm,
             smem,

time: 19.1 us -> 17.6 us (0.921)
  Pallas kernels: 16.9 us -> 16.2 us
  local copies, waits for them, and re-layouts: 1.28 us -> 0.6 us
    pallas_call x1, Pallas kernels: 16.9 us -> 16.2 us  [per_device(): pl.pallas_call(functools.partial(kernel, sizes), out_shape=pltpu.VMEM((ha...]
    unnamed x1, local copies, waits for them, and re-layouts: 1.28 us -> 0.6 us
where the time goes in v3:
time: 17.6 us; the launch traced here: 17.5 us
  Pallas kernels  16.2 us (92%)
  between operations  0.66 us (4%)
  local copies, waits for them, and re-layouts  0.6 us (3%)
    pallas_call x1, Pallas kernels, per_device(): pl.pallas_call(functools.partial(kernel, sizes), out_shape=pltpu.VMEM((ha...  16.2 us
    unnamed x1, local copies, waits for them, and re-layouts  0.6 us

profile of v3, /device:TPU:1, one launch (start us, length us, event | category | flops | bytes accessed | tf_op | source)
XLA Modules:
  0.0 17.5 jit_solution(11119643890127108775)
XLA Ops:
  0.7 16.2 %shard_map.109 = f32[8,128]{1,0:T(8,128)S(1)} custom-call(bf16[16,16,8,128]{3,2,1,0:T(8,128)(2,1)} %bitcast.9, s32[2,2,4]{2,1,0:T(2,128)} %bitcast.13, bf16[128,128]{1,0:T(8,128)(2,1)} %w_lat.1, f32[1,128]{1,0:T(1,128)} %bitcast.14, bf16[1152,128]{1,0:T(8,128)(2,1)} %bitcast.10, bf16[1152,128]{1,0:T(8,128)(2,1)} %bitcast.11, f32[1,128]{1,0:T(1,128)} %bitcast.15, ...), custom_call_target="tpu_custom_call" | custom-call | flops 2264924160 | bytes 4194304 | tf_op jit(solution)/shard_map/pallas_call | solution.py:482
  16.9 0.6 %copy.13 = f32[8,128]{1,0:T(8,128)} copy(f32[8,128]{1,0:T(8,128)S(1)} %shard_map.109) | data formatting | bytes 8192

commit v4 on v3

--- a/solution.py
+++ b/solution.py
@@ -362,8 +362,6 @@
     for date in (0, 1):
         lateral_sides(date)
     phase(0)
-    await_kind(1)
-    phase(1)
 
     tiles = []
     for kind in (0, 1):
@@ -422,8 +420,6 @@
         regrid_row(p, 1)
         return carry
 
-    lax.fori_loop(0, half // 2 + 2, regrid_body, 0)
-
     for copy in conv_copies[1]:
         copy.wait()
     bias_one = vec_one[...]
@@ -437,7 +433,18 @@
                 part = jnp.where(inside(x_mid, 2 * (i + pair) + slot - 1), part, 0.0)
                 put_taps(hid6, i + pair, slot, part, edge, mid - edge)
 
-    dec_one(0, half // 2 + 1)
+    pairs = half // 2 + 2
+    early = pairs - (HALO[1] + 1) // 2
+    first = jnp.where(upper, pairs - early, 0)
+    for i in range(early):
+        regrid_body(first + i, 0)
+    dec_one(jnp.where(upper, pairs - early, 0), early - 1)
+    await_kind(1)
+    phase(1)
+    first = jnp.where(upper, 0, early)
+    for i in range(pairs - early):
+        regrid_body(first + i, 0)
+    dec_one(jnp.where(upper, 0, early - 1), pairs - early)
 
     for copy in conv_copies[2]:
         copy.wait()

time: 17.6 us -> 16.9 us (0.960)
  Pallas kernels: 16.2 us -> 15.5 us
    pallas_call x1, Pallas kernels: 16.2 us -> 15.5 us  [per_device(): pl.pallas_call(functools.partial(kernel, sizes), out_shape=pltpu.VMEM((ha...]
where the time goes in v4:
time: 16.9 us; the launch traced here: 16.7 us
  Pallas kernels  15.5 us (92%)
  between operations  0.66 us (4%)
  local copies, waits for them, and re-layouts  0.6 us (4%)
    pallas_call x1, Pallas kernels, per_device(): pl.pallas_call(functools.partial(kernel, sizes), out_shape=pltpu.VMEM((ha...  15.5 us
    unnamed x1, local copies, waits for them, and re-layouts  0.6 us

profile of v4, /device:TPU:1, one launch (start us, length us, event | category | flops | bytes accessed | tf_op | source)
XLA Modules:
  0.0 16.7 jit_solution(12051511100647677627)
XLA Ops:
  0.7 15.5 %shard_map.109 = f32[8,128]{1,0:T(8,128)S(1)} custom-call(bf16[16,16,8,128]{3,2,1,0:T(8,128)(2,1)} %bitcast.9, s32[2,2,4]{2,1,0:T(2,128)} %bitcast.13, bf16[128,128]{1,0:T(8,128)(2,1)} %w_lat.1, f32[1,128]{1,0:T(1,128)} %bitcast.14, bf16[1152,128]{1,0:T(8,128)(2,1)} %bitcast.10, bf16[1152,128]{1,0:T(8,128)(2,1)} %bitcast.11, f32[1,128]{1,0:T(1,128)} %bitcast.15, ...), custom_call_target="tpu_custom_call" | custom-call | flops 2264924160 | bytes 4194304 | tf_op jit(solution)/shard_map/pallas_call | solution.py:489
  16.1 0.6 %copy.13 = f32[8,128]{1,0:T(8,128)} copy(f32[8,128]{1,0:T(8,128)S(1)} %shard_map.109) | data formatting | bytes 8192
